TPU v7x, 128 devices: a whole 4x4x4 slice. The times are simulated.
128 devices in a mesh: fluid: 8 (over z, core), patch: 16 (over x, y).
Axes of the slice: x: 4, y: 4, z: 4, core: 2. Of those that a mesh axis runs over, the one named last changes fastest.
Arguments:
- contributions: bfloat16 [262144, 256], P(('fluid', 'patch')), may hold values from -6 to 6
- routes: int32 [262144, 1], P(('fluid', 'patch')), may hold values from 0 to 127; in each aligned block of 2048 rows (0 to 2047, 2048 to 4095, ...) at most 32 rows name the same one
- slots: int32 [262144], P(('fluid', 'patch')), may hold values from 0 to 767
- panels: bfloat16 [98304, 12288], P(('fluid', 'patch')), may hold values from -0.0546875 to 0.0546875
Outputs:
- traces: bfloat16 [98304, 256], P(('fluid', 'patch'))
- added_mass: float32 [256, 256], replicated
Inputs may be any that keep to these rules, and one draw needn't show every extreme that they name: `routes`: among the rows of one device, at most 32 name the same owner.
All inputs are finite; a program needn't handle non-finite values.
Results may differ from a plain program's by a relative error of at most 0.0051.
Values may be sent and summed in bfloat16 or wider, within the bound.
A program may use at most 128 MiB of HBM per device.

v0:
```python
import math

import jax
import jax.numpy as jnp
from jax import lax
from jax.sharding import PartitionSpec as P


def shards(contributions, routes, slots, panels):
    node_rows = panels.shape[0]
    row_width = contributions.shape[1]
    fluid_count = lax.axis_size("fluid")
    patch_count = lax.axis_size("patch")
    devices = fluid_count * patch_count
    capacity = 2 * contributions.shape[0] // devices
    target = routes[:, 0]
    onehot_target = (target[:, None] == jnp.arange(devices, dtype=jnp.int32)[None, :]).astype(
        jnp.int32
    )
    earlier = jnp.cumsum(onehot_target, axis=0) - onehot_target
    order_in = jnp.sum(earlier * onehot_target, axis=1)
    position = target * capacity + order_in
    outgoing = (
        jnp.zeros((devices * capacity, row_width), jnp.bfloat16).at[position].set(contributions)
    )
    out_slots = jnp.full((devices * capacity,), node_rows, jnp.int32).at[position].set(slots)
    arrived, arrived_slots = (
        lax.all_to_all(outgoing, ("fluid", "patch"), split_axis=0, concat_axis=0, tiled=True),
        lax.all_to_all(out_slots, ("fluid", "patch"), split_axis=0, concat_axis=0, tiled=True),
    )
    landing = (jnp.arange(node_rows, dtype=jnp.int32)[:, None] == arrived_slots[None, :]).astype(
        jnp.bfloat16
    )
    traces = jnp.dot(landing, arrived, preferred_element_type=jnp.float32).astype(jnp.bfloat16)
    local_wide = traces.astype(jnp.float32)
    coupled = jnp.dot(
        panels,
        lax.all_gather(traces, "patch", axis=0, tiled=True),
        preferred_element_type=jnp.float32,
    )
    partial_mass = lax.dot_general(
        local_wide, coupled, (((0,), (0,)), ((), ())), precision=lax.Precision.HIGHEST
    )
    summed_mass = lax.psum(partial_mass, ("fluid", "patch"))
    factor = 0.5 / math.sqrt(node_rows * devices)
    added_mass = (summed_mass + summed_mass.T) * factor
    return (traces, added_mass)


def solution(mesh):
    placed = (
        P(("fluid", "patch"), None),
        P(("fluid", "patch"), None),
        P(("fluid", "patch")),
        P(("fluid", "patch"), None),
    )
    return jax.shard_map(
        shards,
        mesh=mesh,
        in_specs=placed,
        out_specs=(P(("fluid", "patch"), None), P()),
        check_vma=False,
    )
```

profile of v0, /device:TPU:1, one launch (start us, length us, event | category | flops | bytes accessed | tf_op | source)
XLA Modules:
  0.0 304.8 jit_solution(17012131078137173378)
XLA Ops:
  7.2 0.0 copy-start.1
  7.2 0.9 copy.11
  8.0 0.3 fusion.7
  8.4 0.1 broadcast_add_fusion
  8.5 0.3 copy.12
  8.9 0.0 copy-done.1
  8.9 0.6 fusion.4
  9.5 8.2 %scatter_custom_fusion = s32[4096]{0:T(1024)S(1)} fusion(s32[2048]{0:T(1024)S(1)} %bitcast.33, s32[2048]{0:T(1024)} %param.6, s32[]{:T(128)} %constant.6.clone.1), kind=kCustom, calls=%fused_computation.21 | custom fusion | bytes 16896 | tf_op jit(solution)/shard_map/scatter | solution.py:26
  17.8 0.7 all_to_all.14
  18.5 11.5 %all-to-all-start = ((s32[128,32,1]{1,2,0:T(1,128)}), s32[128,32,1]{1,2,0:T(1,128)S(1)}, u32[]{:S(2)}, u32[]{:S(2)}) async-start(s32[128,32,1]{1,2,0:T(1,128)} %bitcast.7), calls=%async_computation | async-start | bytes 131072 | tf_op jit(solution)/shard_map/all_to_all | solution.py:29
  30.0 11.3 %scatter_custom_fusion.1 = bf16[4096,256]{1,0:T(8,128)(2,1)} fusion(s32[2048]{0:T(1024)S(1)} %bitcast.34, bf16[2048,256]{1,0:T(8,128)(2,1)} %param.4, bf16[]{:T(256)} %constant.5.clone.1), kind=kCustom, calls=%fused_computation.9 | custom fusion | bytes 2097664 | tf_op jit(solution)/shard_map/scatter | solution.py:24
  41.3 0.0 all-to-all-done
  41.3 9.8 %all-to-all-start.1 = ((bf16[128,32,256]{2,1,0:T(8,128)(2,1)}), bf16[128,32,256]{2,1,0:T(8,128)(2,1)S(1)}, u32[]{:S(2)}, u32[]{:S(2)}) async-start(bf16[128,32,256]{2,1,0:T(8,128)(2,1)} %bitcast.8), calls=%async_computation.1 | async-start | bytes 4194304 | tf_op jit(solution)/shard_map/all_to_all | solution.py:28
  51.0 0.0 all-gather.2.cloned.1.call-start
  51.1 0.5 broadcast.34
  51.6 0.8 reduce.3
  52.4 0.1 eq.49
  52.5 28.3 %all-to-all-done.1 = bf16[128,32,256]{2,1,0:T(8,128)(2,1)S(1)} async-done(((bf16[128,32,256]{2,1,0:T(8,128)(2,1)}), bf16[128,32,256]{2,1,0:T(8,128)(2,1)S(1)}, u32[]{:S(2)}, u32[]{:S(2)}) %all-to-all-start.1) | async-done | bytes 2097184 | tf_op jit(solution)/shard_map/all_to_all | solution.py:28
  80.8 2.8 fusion.2
  83.6 0.0 all-gather.2.cloned.1.call-update
  83.6 0.0 copy-start
  83.6 0.2 all-reduce.2.cloned.1.call-start
  83.9 57.3 %all-gather.2.cloned.1.call-done = bf16[12288,256]{1,0:T(8,128)(2,1)} async-done(((bf16[768,256]{1,0:T(8,128)(2,1)}), bf16[12288,256]{1,0:T(8,128)(2,1)}) %all-gather.2.cloned.1.call-update) | async-done | bytes 6291472 | tf_op jit(solution)/shard_map/all_gather | solution.py:38
  141.2 11.1 %fusion.13 = f32[256,768]{1,0:T(8,128)S(1)} fusion(bf16[12288,256]{1,0:T(8,128)(2,1)} %all-gather.2.cloned.1.call-done, bf16[768,12288]{1,0:T(8,128)(2,1)} %param.7), kind=kOutput, calls=%fused_computation.23 | convolution fusion | flops 4831838208 | bytes 25952256 | tf_op jit(solution)/shard_map/dot_general | solution.py:36
  152.3 0.0 copy-done
  152.4 1.4 fusion.14
  153.7 0.0 all-reduce.2.cloned.1.call-update
  153.7 141.5 %all-reduce.2.cloned.1.call-done = f32[256,256]{1,0:T(8,128)} async-done(((f32[256,256]{1,0:T(8,128)}), f32[256,256]{1,0:T(8,128)}) %all-reduce.2.cloned.1.call-update) | async-done | bytes 262160 | tf_op jit(solution)/shard_map/psum | solution.py:44
  295.2 1.1 copy.14
  296.3 1.7 fusion.10
  (4 shorter events, 0.1 us)
Async XLA Ops:
  7.2 1.7 copy-start.1
  18.5 22.8 %all-to-all-start = ((s32[128,32,1]{1,2,0:T(1,128)}), s32[128,32,1]{1,2,0:T(1,128)S(1)}, u32[]{:S(2)}, u32[]{:S(2)}) async-start(s32[128,32,1]{1,2,0:T(1,128)} %bitcast.7), calls=%async_computation | async-start | bytes 131072 | tf_op jit(solution)/shard_map/all_to_all | solution.py:29
  41.3 39.5 %all-to-all-start.1 = ((bf16[128,32,256]{2,1,0:T(8,128)(2,1)}), bf16[128,32,256]{2,1,0:T(8,128)(2,1)S(1)}, u32[]{:S(2)}, u32[]{:S(2)}) async-start(bf16[128,32,256]{2,1,0:T(8,128)(2,1)} %bitcast.8), calls=%async_computation.1 | async-start | bytes 4194304 | tf_op jit(solution)/shard_map/all_to_all | solution.py:28
  51.0 90.2 %all-gather.2.cloned.1.call-start = ((), (), s32[]{:S(2)}) async-start(), calls=%async_computation.2 | async-start | bytes 6684672 | tf_op jit(solution)/shard_map/all_gather | solution.py:38
  83.6 68.7 %copy-start = (bf16[768,256]{1,0:T(8,128)(2,1)S(1)}, bf16[768,256]{1,0:T(8,128)(2,1)}, u32[]{:S(2)}) copy-start(bf16[768,256]{1,0:T(8,128)(2,1)} %fusion.2) | copy-start | bytes 1179652
  83.6 211.6 %all-reduce.2.cloned.1.call-start = ((), (), s32[]{:S(2)}) async-start(), calls=%async_computation.3 | async-start | bytes 524288 | tf_op jit(solution)/shard_map/psum | solution.py:44
Sparse Core Ops, SparseCore 0:
  83.8 57.4 all-gather.1
  153.9 141.3 all-reduce.1
where the time goes:
time: 305 us
  waiting for transfers between devices  227 us (74%)
  local copies, waits for them, and re-layouts  23.1 us (8%)
  starting transfers between devices  21.5 us (7%)
  matrix products  15.3 us (5%)
  between operations  14.2 us (5%)
  other arithmetic  3.59 us (1%)
    psum x1, waiting for transfers between devices, shards(): summed_mass = lax.psum(partial_mass, ('fluid', 'patch'))  141 us
    all_gather x1, waiting for transfers between devices, shards(): lax.all_gather(traces, 'patch', axis=0, tiled=True)  57.3 us
    all_to_all x1, waiting for transfers between devices, shards(): lax.all_to_all(outgoing, ('fluid', 'patch'), split_axis=0, concat_axis=0,...  28.3 us
    all_to_all x1, starting transfers between devices, shards(): lax.all_to_all(out_slots, ('fluid', 'patch'), split_axis=0, concat_axis=0...  11.5 us
    scatter x1, local copies, waits for them, and re-layouts, shards(): jnp.zeros((devices * capacity, row_width), jnp.bfloat16).at[position]  11.3 us
    dot_general x1, matrix products, shards(): jnp.dot(panels, lax.all_gather(traces, 'patch', axis=0, tiled=True), pref...  11.1 us
    all_to_all x1, starting transfers between devices, shards(): lax.all_to_all(outgoing, ('fluid', 'patch'), split_axis=0, concat_axis=0,...  9.76 us
    scatter x1, local copies, waits for them, and re-layouts, shards(): jnp.full((devices * capacity,), node_rows, jnp.int32).at[position]  8.23 us
  transfers between devices with their start and end apart: 4, of which 3 were waited for; matrix products, arithmetic and copies ran while one was open for 4% of the time, Pallas kernels for 0%

commit v1 on v0

v1 whole, which is shorter than its diff:
```python
import functools
import math

import jax
import jax.numpy as jnp
from jax import lax
from jax.experimental import pallas as pl
from jax.experimental.pallas import tpu as pltpu
from jax.sharding import PartitionSpec as P

MESH = pl.DeviceIdType.MESH
SIDE = 4
COLUMN = 8
PLANE = 16
CAP = 32
STRIDE = 5


def where_am_i():
    f, p = lax.axis_index("fluid"), lax.axis_index("patch")
    return f // 2, lax.rem(f, 2), p // SIDE, lax.rem(p, SIDE)


def shifted(column_step, plane_step, sign=1):
    z, c, x, y = where_am_i()
    dz, dc = column_step // 2, column_step % 2
    dx, dy = plane_step // SIDE, plane_step % SIDE
    if sign < 0:
        dz, dx, dy = SIDE - dz, SIDE - dx, SIDE - dy
    return (
        lax.rem(z + dz, SIDE) * 2 + lax.rem(c + dc, 2),
        lax.rem(x + dx, SIDE) * SIDE + lax.rem(y + dy, SIDE),
    )


def kernel(
    factor, contributions, routes, slots, panels, traces, mass,
    out_rows, in_rows, onehot, position, slot_out, column_slots, plane_out, plane_slots, landed,
    gathered, panel_v, coupled, share, reduce_in, column_in, full,
    row_send, row_recv, slot_send, slot_recv, plane_send, plane_recv, gather_send, gather_recv, panel_sem,
    reduce_send, reduce_recv, column_send, column_recv, full_send, full_recv,
):
    f32, bf16, i32 = jnp.float32, jnp.bfloat16, jnp.int32
    f, p = lax.axis_index("fluid"), lax.axis_index("patch")
    z, c, x, y = where_am_i()
    rows = contributions.shape[0]
    nodes = traces.shape[0]
    width = traces.shape[1]
    half, piece = nodes // 2, nodes // 4

    barrier = pltpu.get_barrier_semaphore()

    @pl.loop(1, COLUMN * PLANE)
    def _(i):
        pl.semaphore_signal(barrier, inc=1, device_id=shifted(i // PLANE, i % PLANE), device_id_type=MESH)

    panel_copies = []
    for s in range(PLANE):
        dx, dy = s // SIDE, s % SIDE
        owner = lax.rem(x + SIDE - dx, SIDE) * SIDE + lax.rem(y + SIDE - dy, SIDE)
        copy = pltpu.make_async_copy(
            panels.at[:, pl.ds(pl.multiple_of(owner * nodes, 128), nodes)], panel_v.at[s], panel_sem.at[s]
        )
        copy.start()
        panel_copies.append(copy)

    to = routes[...]
    to_f, to_p = to >> 4, to & 15
    dz, dc = ((to_f >> 1) - z) & 3, ((to_f & 1) - c) & 1
    dx, dy = ((to_p >> 2) - x) & 3, ((to_p & 3) - y) & 3
    step_column, step_plane = dz * 2 + dc, dx * 4 + dy
    label = step_column * PLANE + step_plane
    onehot[...] = (lax.broadcasted_iota(i32, (128, rows), 0) == label).astype(bf16)
    block = 256
    upper = (
        lax.broadcasted_iota(i32, (block, block), 0) < lax.broadcasted_iota(i32, (block, block), 1)
    ).astype(bf16)
    seen = jnp.zeros((128, 1), f32)
    orders = []
    for b in range(rows // block):
        mine = onehot[:, b * block:(b + 1) * block]
        before = jnp.dot(mine, upper, preferred_element_type=f32) + seen
        wide = mine.astype(f32)
        orders.append(jnp.sum(wide * before, axis=0, keepdims=True))
        seen = seen + jnp.sum(wide, axis=1, keepdims=True)
    order = jnp.concatenate(orders, axis=1).astype(i32)
    turn = (step_plane - STRIDE * step_column) & 15
    position[...] = (turn * COLUMN + step_column) * CAP + order

    value = slots[...] + 1
    lane_order = lax.broadcasted_iota(i32, (128, rows), 0) & (CAP - 1)
    hit = lane_order == order
    nt = (((1,), (1,)), ((), ()))
    high = jnp.where(hit, (value >> 5).astype(f32), 0.0).astype(bf16)
    table = lax.dot_general(onehot[...], high, nt, preferred_element_type=f32) * 32.0
    low = jnp.where(hit, (value & 31).astype(f32), 0.0).astype(bf16)
    table = table + lax.dot_general(onehot[...], low, nt, preferred_element_type=f32)
    lane_group = lax.broadcasted_iota(i32, (128, 128), 1) >> 5
    row_group = (lax.broadcasted_iota(i32, (128, 128), 0) >> 4) & 3
    slot_out[...] = jnp.where(lane_group == row_group, table, 0.0).astype(i32)
    column_slots[0] = slot_out[0:PLANE]

    pl.semaphore_wait(barrier, COLUMN * PLANE - 1)

    slot_copies = []
    for w in range(1, COLUMN):
        copy = pltpu.make_async_remote_copy(
            src_ref=slot_out.at[pl.ds(w * PLANE, PLANE)], dst_ref=column_slots.at[w],
            send_sem=slot_send.at[w], recv_sem=slot_recv.at[w], device_id=shifted(w, 0), device_id_type=MESH,
        )
        copy.start()
        slot_copies.append(copy)

    def build(kk):
        i = lax.broadcasted_iota(i32, (256, 1), 0)
        pick = (kk * 256 + i == position[...]).astype(bf16)
        made = jnp.dot(pick, contributions[...], preferred_element_type=f32).astype(bf16)
        out_rows[pl.ds(pl.multiple_of(kk * 256, 256), 256), :] = made

    def row_copy(kk, w):
        at = pl.ds(pl.multiple_of(kk * 256 + w * CAP, CAP), CAP)
        return pltpu.make_async_remote_copy(
            src_ref=out_rows.at[at], dst_ref=in_rows.at[at],
            send_sem=row_send, recv_sem=row_recv.at[kk],
            device_id=shifted(w, lax.rem(kk + STRIDE * w, PLANE)), device_id_type=MESH,
        )

    @pl.loop(1, PLANE)
    def _(kk):
        build(kk)
        for w in range(COLUMN):
            row_copy(kk, w).start()

    build(0)
    for w in range(1, COLUMN):
        row_copy(0, w).start()
    in_rows[0:CAP, :] = out_rows[0:CAP, :]

    for copy in slot_copies:
        copy.wait()
    first = column_slots[0] + column_slots[1] + column_slots[2] + column_slots[3]
    second = column_slots[4] + column_slots[5] + column_slots[6] + column_slots[7]
    sub = lax.broadcasted_iota(i32, (PLANE, 8, 128), 1)
    plane_out[...] = jnp.where(sub < 4, first[:, None, :], second[:, None, :])
    plane_slots[0] = plane_out[0]
    plane_copies = []
    for s in range(1, PLANE):
        copy = pltpu.make_async_remote_copy(
            src_ref=plane_out.at[s], dst_ref=plane_slots.at[s],
            send_sem=plane_send.at[s], recv_sem=plane_recv.at[s], device_id=shifted(0, s), device_id_type=MESH,
        )
        copy.start()
        plane_copies.append(copy)
    for copy in plane_copies:
        copy.wait()

    landed[...] = jnp.zeros_like(landed)

    def land(kk):
        group = lax.broadcasted_iota(i32, (1, 128), 1) >> 5
        parts = []
        for side in range(2):
            row = jnp.zeros((1, 128), i32)
            for k in range(4):
                w = side * 4 + k
                got = plane_slots[lax.rem(kk + STRIDE * w, PLANE), pl.ds(side * 4, 1), :]
                row = row + jnp.where(group == k, got, 0)
            parts.append(row)
        names = jnp.concatenate(parts, axis=1) - 1
        spread = (lax.broadcasted_iota(i32, (nodes, 256), 0) == names).astype(bf16)
        landed[...] += jnp.dot(
            spread, in_rows[pl.ds(pl.multiple_of(kk * 256, 256), 256), :], preferred_element_type=f32
        )

    def arrival(kk, start, count):
        at = pl.ds(start, count)
        return pltpu.make_async_remote_copy(
            src_ref=in_rows.at[at], dst_ref=in_rows.at[at],
            send_sem=row_send, recv_sem=row_recv.at[kk], device_id=(f, p), device_id_type=MESH,
        )

    @pl.loop(1, PLANE)
    def _(kk):
        arrival(kk, pl.multiple_of(kk * 256, 256), 256).wait_recv()
        land(kk)

    arrival(0, CAP, 256 - CAP).wait_recv()
    land(0)
    own = landed[...].astype(bf16)
    gathered[0] = own

    sent = []

    def pass_on(axis, direction, source, start, count, sem):
        dx, dy = source
        if axis == 0:
            dx = (dx + direction) % SIDE
            device = (f, lax.rem(x + direction + SIDE, SIDE) * SIDE + y)
        else:
            dy = (dy + direction) % SIDE
            device = (f, x * SIDE + lax.rem(y + direction + SIDE, SIDE))
        at = pl.ds(start, count)
        copy = pltpu.make_async_remote_copy(
            src_ref=gathered.at[source[0] * SIDE + source[1], at], dst_ref=gathered.at[dx * SIDE + dy, at],
            send_sem=gather_send, recv_sem=gather_recv.at[(dx * SIDE + dy) * 4 + sem],
            device_id=device, device_id_type=MESH,
        )
        copy.start()
        sent.append(count)

    def await_piece(source, start, count, sem):
        s = source[0] * SIDE + source[1]
        at = pl.ds(start, count)
        pltpu.make_async_remote_copy(
            src_ref=gathered.at[s, at], dst_ref=gathered.at[s, at],
            send_sem=gather_send, recv_sem=gather_recv.at[s * 4 + sem], device_id=(f, p), device_id_type=MESH,
        ).wait_recv()

    def at(lead, a, b):
        return (a, b) if lead == 0 else (b, a)

    def send_half(lead, axis, direction, source):
        pass_on(axis, direction, source, lead * half, half, lead * 2)

    def send_piece(lead, axis, direction, source, k):
        pass_on(axis, direction, source, lead * half + k * piece, piece, lead * 2 + k)

    def wait_half(lead, source):
        await_piece(source, lead * half, half, lead * 2)

    def wait_piece(lead, source, k):
        await_piece(source, lead * half + k * piece, piece, lead * 2 + k)

    def multiply(s, start, count):
        coupled[...] += jnp.dot(
            panel_v[s, :, pl.ds(start, count)], gathered[s, pl.ds(start, count), :], preferred_element_type=f32
        )

    for lead in (0, 1):
        for direction in (1, -1):
            send_half(lead, lead, direction, (0, 0))
            send_half(lead, 1 - lead, direction, (0, 0))
    traces[...] = own
    coupled[...] = jnp.zeros_like(coupled)
    for copy in panel_copies:
        copy.wait()
    multiply(0, 0, nodes)

    def multiply_halves(places):
        for lead, place in places:
            multiply(place[0] * SIDE + place[1], lead * half, half)

    for k, a, direction in ((0, 1, 1), (1, 3, -1)):
        for lead in (0, 1):
            place = at(lead, a, 0)
            wait_half(lead, place)
            send_piece(lead, lead, direction, place, k)
            send_half(lead, 1 - lead, 1, place)
            send_half(lead, 1 - lead, -1, place)
    for k, b, direction in ((0, 1, 1), (1, 3, -1)):
        for lead in (0, 1):
            place = at(lead, 0, b)
            wait_half(lead, place)
            send_piece(lead, 1 - lead, direction, place, k)
    multiply_halves([(lead, at(lead, a, b)) for a, b in ((1, 0), (3, 0), (0, 1), (0, 3)) for lead in (0, 1)])
    for k in (0, 1):
        for lead in (0, 1):
            place = at(lead, 2, 0)
            wait_piece(lead, place, k)
            send_piece(lead, 1 - lead, 1, place, k)
            send_piece(lead, 1 - lead, -1, place, k)
    multiply_halves([(lead, at(lead, 2, 0)) for lead in (0, 1)])
    for a in (1, 3):
        for k, b, direction in ((0, 1, 1), (1, 3, -1)):
            for lead in (0, 1):
                place = at(lead, a, b)
                wait_half(lead, place)
                send_piece(lead, 1 - lead, direction, place, k)
        multiply_halves([(lead, at(lead, a, b)) for b in (1, 3) for lead in (0, 1)])
    for k in (0, 1):
        for lead in (0, 1):
            wait_piece(lead, at(lead, 0, 2), k)
    multiply_halves([(lead, at(lead, 0, 2)) for lead in (0, 1)])
    for lead in (0, 1):
        place = at(lead, 2, 1)
        wait_piece(lead, place, 0)
        send_piece(lead, 1 - lead, 1, place, 0)
        place = at(lead, 2, 3)
        wait_piece(lead, place, 1)
        send_piece(lead, 1 - lead, -1, place, 1)
    for lead in (0, 1):
        wait_piece(lead, at(lead, 2, 1), 1)
        wait_piece(lead, at(lead, 2, 3), 0)
    multiply_halves([(lead, at(lead, 2, b)) for b in (1, 3) for lead in (0, 1)])
    for a in (1, 3):
        for k in (0, 1):
            for lead in (0, 1):
                wait_piece(lead, at(lead, a, 2), k)
        multiply_halves([(lead, at(lead, a, 2)) for lead in (0, 1)])
    for k in (0, 1):
        for lead in (0, 1):
            wait_piece(lead, at(lead, 2, 2), k)
    multiply_halves([(lead, at(lead, 2, 2)) for lead in (0, 1)])

    tn = (((0,), (0,)), ((), ()))
    top = coupled[...].astype(bf16)
    rest = (coupled[...] - top.astype(f32)).astype(bf16)
    share[...] = lax.dot_general(own, top, tn, preferred_element_type=f32) + lax.dot_general(
        own, rest, tn, preferred_element_type=f32
    )

    strip = width // PLANE
    copies = []
    for s in range(1, PLANE):
        device = shifted(0, s)
        copy = pltpu.make_async_remote_copy(
            src_ref=share.at[pl.ds(pl.multiple_of(device[1] * strip, strip), strip)], dst_ref=reduce_in.at[s],
            send_sem=reduce_send.at[s], recv_sem=reduce_recv.at[s], device_id=device, device_id_type=MESH,
        )
        copy.start()
        copies.append(copy)
    total = share[pl.ds(pl.multiple_of(p * strip, strip), strip), :]
    for s, copy in enumerate(copies):
        copy.wait()
        total = total + reduce_in[s + 1]
    column_in[f] = total
    copies = []
    for w in range(1, COLUMN):
        copy = pltpu.make_async_remote_copy(
            src_ref=column_in.at[f], dst_ref=column_in.at[f],
            send_sem=column_send.at[w], recv_sem=column_recv.at[w], device_id=shifted(w, 0), device_id_type=MESH,
        )
        copy.start()
        copies.append(copy)
    for copy in copies:
        copy.wait()
    total = column_in[0]
    for w in range(1, COLUMN):
        total = total + column_in[w]
    mine = pl.ds(pl.multiple_of(p * strip, strip), strip)
    full[mine, :] = total
    copies = []
    for s in range(1, PLANE):
        copy = pltpu.make_async_remote_copy(
            src_ref=full.at[mine], dst_ref=full.at[mine],
            send_sem=full_send.at[s], recv_sem=full_recv.at[s], device_id=shifted(0, s), device_id_type=MESH,
        )
        copy.start()
        copies.append(copy)
    for copy in copies:
        copy.wait()
    mass[...] = (full[...] + full[...].T) * factor

    everything = pl.ds(CAP, rows * 2 - CAP)
    pltpu.make_async_remote_copy(
        src_ref=out_rows.at[everything], dst_ref=out_rows.at[everything],
        send_sem=row_send, recv_sem=row_recv.at[0], device_id=(f, p), device_id_type=MESH,
    ).wait_send()
    assert sum(sent) % nodes == 0
    blocks = pl.ds(0, sum(sent) // nodes)
    pltpu.make_async_remote_copy(
        src_ref=gathered.at[blocks], dst_ref=gathered.at[blocks],
        send_sem=gather_send, recv_sem=gather_recv.at[0], device_id=(f, p), device_id_type=MESH,
    ).wait_send()


def shards(contributions, routes, slots, panels):
    rows, width = contributions.shape
    nodes = panels.shape[0]
    devices = lax.axis_size("fluid") * lax.axis_size("patch")
    bf16, f32, i32 = jnp.bfloat16, jnp.float32, jnp.int32
    strip = width // PLANE
    vmem = pl.BlockSpec(memory_space=pltpu.VMEM)
    dma = pltpu.SemaphoreType.DMA
    return pl.pallas_call(
        functools.partial(kernel, 0.5 / math.sqrt(nodes * devices)),
        out_shape=(
            jax.ShapeDtypeStruct((nodes, width), bf16),
            jax.ShapeDtypeStruct((width, width), f32),
        ),
        in_specs=[vmem, vmem, vmem, pl.BlockSpec(memory_space=pl.ANY)],
        out_specs=(vmem, vmem),
        scratch_shapes=[
            pltpu.VMEM((2 * rows, width), bf16),
            pltpu.VMEM((2 * rows, width), bf16),
            pltpu.VMEM((128, rows), bf16),
            pltpu.VMEM((1, rows), i32),
            pltpu.VMEM((128, 128), i32),
            pltpu.VMEM((COLUMN, PLANE, 128), i32),
            pltpu.VMEM((PLANE, 8, 128), i32),
            pltpu.VMEM((PLANE, 8, 128), i32),
            pltpu.VMEM((nodes, width), f32),
            pltpu.VMEM((PLANE, nodes, width), bf16),
            pltpu.VMEM((PLANE, nodes, nodes), bf16),
            pltpu.VMEM((nodes, width), f32),
            pltpu.VMEM((width, width), f32),
            pltpu.VMEM((PLANE, strip, width), f32),
            pltpu.VMEM((COLUMN, strip, width), f32),
            pltpu.VMEM((width, width), f32),
            dma, dma((PLANE,)), dma((COLUMN,)), dma((COLUMN,)), dma((PLANE,)), dma((PLANE,)),
            dma, dma((PLANE * 4,)), dma((PLANE,)),
            dma((PLANE,)), dma((PLANE,)), dma((COLUMN,)), dma((COLUMN,)), dma((PLANE,)), dma((PLANE,)),
        ],
        compiler_params=pltpu.CompilerParams(
            collective_id=0, has_side_effects=True, vmem_limit_bytes=60 * 1024 * 1024
        ),
        cost_estimate=pl.CostEstimate(
            flops=2 * nodes * PLANE * nodes * width, bytes_accessed=nodes * nodes * PLANE * 2, transcendentals=0
        ),
    )(contributions, routes.reshape(1, rows), slots.reshape(1, rows), panels)


def solution(mesh):
    placed = (
        P(("fluid", "patch"), None),
        P(("fluid", "patch"), None),
        P(("fluid", "patch")),
        P(("fluid", "patch"), None),
    )
    return jax.shard_map(
        shards,
        mesh=mesh,
        in_specs=placed,
        out_specs=(P(("fluid", "patch"), None), P()),
        check_vma=False,
    )
```

time: 305 us -> 106 us (0.35)
  waiting for transfers between devices: 227 us -> 0 us
  Pallas kernels: 0 us -> 102 us
  starting transfers between devices: 21.5 us -> 0 us
  local copies, waits for them, and re-layouts: 23.1 us -> 3.44 us
  matrix products: 15.3 us -> 0 us
  between operations: 14.2 us -> 0.64 us
  other arithmetic: 3.59 us -> 0 us
    psum x1 -> x0, waiting for transfers between devices: 141 us -> none  [shards(): summed_mass = lax.psum(partial_mass, ('fluid', 'patch'))]
    pallas_call x0 -> x1, Pallas kernels: none -> 102 us  [shards(): pl.pallas_call(functools.partial(kernel, 0.5 / math.sqrt(nodes * devices)...]
    all_gather x1 -> x0, waiting for transfers between devices: 57.3 us -> none  [shards(): lax.all_gather(traces, 'patch', axis=0, tiled=True)]
    all_to_all x2 -> x0, waiting for transfers between devices: 28.3 us -> none  [the longest x1 28.3 us: shards(): lax.all_to_all(outgoing, ('fluid', 'patch'), split_axis=0, concat_axis=0,...]
    all_to_all x2 -> x0, starting transfers between devices: 21.3 us -> none  [the longest x1 11.5 us: shards(): lax.all_to_all(out_slots, ('fluid', 'patch'), split_axis=0, concat_axis=0...]
    scatter x2 -> x0, local copies, waits for them, and re-layouts: 19.5 us -> none  [the longest x1 11.3 us: shards(): jnp.zeros((devices * capacity, row_width), jnp.bfloat16).at[position]]
    dot_general x3 -> x0, matrix products: 15.3 us -> none  [the longest x1 11.1 us: shards(): jnp.dot(panels, lax.all_gather(traces, 'patch', axis=0, tiled=True), pref...]
    unnamed x4 -> x2, local copies, waits for them, and re-layouts: 0.01 us -> 3.44 us
  transfers between devices with their start and end apart: 4 -> 0, of which waited for: 3 -> 0; matrix products, arithmetic and copies ran while one was open for 4% -> 0% of each run, Pallas kernels for 0% -> 0%
where the time goes in v1:
time: 106 us
  Pallas kernels  102 us (96%)
  local copies, waits for them, and re-layouts  3.44 us (3%)
    pallas_call x1, Pallas kernels, shards(): pl.pallas_call(functools.partial(kernel, 0.5 / math.sqrt(nodes * devices)...  102 us
    unnamed x2, local copies, waits for them, and re-layouts  3.44 us

profile of v1, /device:TPU:1, one launch (start us, length us, event | category | flops | bytes accessed | tf_op | source)
XLA Modules:
  0.0 105.9 jit_solution(10019104022387821937)
XLA Ops:
  0.6 101.8 %shard_map.59 = (bf16[768,256]{1,0:T(8,128)(2,1)}, f32[256,256]{1,0:T(8,128)}) custom-call(bf16[2048,256]{1,0:T(8,128)(2,1)} %contributions.1, s32[1,2048]{1,0:T(1,128)} %bitcast.2, s32[1,2048]{1,0:T(1,128)} %bitcast.3, bf16[768,12288]{1,0:T(8,128)(2,1)} %panels.1), custom_call_target="tpu_custom_call" | custom-call | flops 4831838208 | bytes 18874368 | tf_op jit(solution)/shard_map/pallas_call | solution.py:375
  102.4 1.8 %copy.8 = bf16[768,256]{1,0:T(8,128)(2,1)} copy(bf16[768,256]{1,0:T(8,128)(2,1)} %get-tuple-element.4) | data formatting | bytes 786432
  104.2 1.7 %copy.9 = f32[256,256]{1,0:T(8,128)} copy(f32[256,256]{1,0:T(8,128)} %get-tuple-element.5) | data formatting | bytes 524288

commit v2 on v1

--- a/solution.py
+++ b/solution.py
@@ -34,11 +34,11 @@
 
 
 def kernel(
-    factor, contributions, routes, slots, panels, traces, mass,
+    contributions, routes, slots, panels, traces, mass,
     out_rows, in_rows, onehot, position, slot_out, column_slots, plane_out, plane_slots, landed,
-    gathered, panel_v, coupled, share, reduce_in, column_in, full,
+    gathered, panel_v, coupled, own_t, share, other, reduce_in, column_in, full, entered,
     row_send, row_recv, slot_send, slot_recv, plane_send, plane_recv, gather_send, gather_recv, panel_sem,
-    reduce_send, reduce_recv, column_send, column_recv, full_send, full_recv,
+    core_send, core_recv, reduce_send, reduce_recv, column_send, column_recv, full_send, full_recv,
 ):
     f32, bf16, i32 = jnp.float32, jnp.bfloat16, jnp.int32
     f, p = lax.axis_index("fluid"), lax.axis_index("patch")
@@ -50,9 +50,10 @@
 
     barrier = pltpu.get_barrier_semaphore()
 
-    @pl.loop(1, COLUMN * PLANE)
-    def _(i):
-        pl.semaphore_signal(barrier, inc=1, device_id=shifted(i // PLANE, i % PLANE), device_id_type=MESH)
+    for s in range(1, PLANE):
+        pl.semaphore_signal(barrier, inc=1, device_id=shifted(0, s), device_id_type=MESH)
+    for w in range(1, COLUMN):
+        pl.semaphore_signal(barrier, inc=1, device_id=shifted(w, 0), device_id_type=MESH)
 
     panel_copies = []
     for s in range(PLANE):
@@ -72,6 +73,10 @@
     label = step_column * PLANE + step_plane
     onehot[...] = (lax.broadcasted_iota(i32, (128, rows), 0) == label).astype(bf16)
     block = 256
+    pl.semaphore_wait(barrier, PLANE + COLUMN - 2)
+    for w in range(1, COLUMN):
+        pl.semaphore_signal(entered, inc=1, device_id=shifted(w, 0), device_id_type=MESH)
+
     upper = (
         lax.broadcasted_iota(i32, (block, block), 0) < lax.broadcasted_iota(i32, (block, block), 1)
     ).astype(bf16)
@@ -87,6 +92,31 @@
     turn = (step_plane - STRIDE * step_column) & 15
     position[...] = (turn * COLUMN + step_column) * CAP + order
 
+    pl.semaphore_wait(entered, COLUMN - 1)
+
+    def build(kk):
+        i = lax.broadcasted_iota(i32, (256, 1), 0)
+        pick = (kk * 256 + i == position[...]).astype(bf16)
+        made = jnp.dot(pick, contributions[...], preferred_element_type=f32).astype(bf16)
+        out_rows[pl.ds(pl.multiple_of(kk * 256, 256), 256), :] = made
+
+    def row_copy(kk, w):
+        at = pl.ds(pl.multiple_of(kk * 256 + w * CAP, CAP), CAP)
+        return pltpu.make_async_remote_copy(
+            src_ref=out_rows.at[at], dst_ref=in_rows.at[at],
+            send_sem=row_send, recv_sem=row_recv.at[kk],
+            device_id=shifted(w, lax.rem(kk + STRIDE * w, PLANE)), device_id_type=MESH,
+        )
+
+    def send_rows(first, last):
+        @pl.loop(first, last)
+        def _(kk):
+            build(kk)
+            for w in range(COLUMN):
+                row_copy(kk, w).start()
+
+    send_rows(1, 3)
+
     value = slots[...] + 1
     lane_order = lax.broadcasted_iota(i32, (128, rows), 0) & (CAP - 1)
     hit = lane_order == order
@@ -100,8 +130,6 @@
     slot_out[...] = jnp.where(lane_group == row_group, table, 0.0).astype(i32)
     column_slots[0] = slot_out[0:PLANE]
 
-    pl.semaphore_wait(barrier, COLUMN * PLANE - 1)
-
     slot_copies = []
     for w in range(1, COLUMN):
         copy = pltpu.make_async_remote_copy(
@@ -111,30 +139,7 @@
         copy.start()
         slot_copies.append(copy)
 
-    def build(kk):
-        i = lax.broadcasted_iota(i32, (256, 1), 0)
-        pick = (kk * 256 + i == position[...]).astype(bf16)
-        made = jnp.dot(pick, contributions[...], preferred_element_type=f32).astype(bf16)
-        out_rows[pl.ds(pl.multiple_of(kk * 256, 256), 256), :] = made
-
-    def row_copy(kk, w):
-        at = pl.ds(pl.multiple_of(kk * 256 + w * CAP, CAP), CAP)
-        return pltpu.make_async_remote_copy(
-            src_ref=out_rows.at[at], dst_ref=in_rows.at[at],
-            send_sem=row_send, recv_sem=row_recv.at[kk],
-            device_id=shifted(w, lax.rem(kk + STRIDE * w, PLANE)), device_id_type=MESH,
-        )
-
-    @pl.loop(1, PLANE)
-    def _(kk):
-        build(kk)
-        for w in range(COLUMN):
-            row_copy(kk, w).start()
-
-    build(0)
-    for w in range(1, COLUMN):
-        row_copy(0, w).start()
-    in_rows[0:CAP, :] = out_rows[0:CAP, :]
+    send_rows(3, 9)
 
     for copy in slot_copies:
         copy.wait()
@@ -151,6 +156,13 @@
         )
         copy.start()
         plane_copies.append(copy)
+
+    send_rows(9, PLANE)
+    build(0)
+    for w in range(1, COLUMN):
+        row_copy(0, w).start()
+    in_rows[0:CAP, :] = out_rows[0:CAP, :]
+
     for copy in plane_copies:
         copy.wait()
 
@@ -241,6 +253,7 @@
             send_half(lead, lead, direction, (0, 0))
             send_half(lead, 1 - lead, direction, (0, 0))
     traces[...] = own
+    own_t[...] = own.T
     coupled[...] = jnp.zeros_like(coupled)
     for copy in panel_copies:
         copy.wait()
@@ -302,14 +315,25 @@
             wait_piece(lead, at(lead, 2, 2), k)
     multiply_halves([(lead, at(lead, 2, 2)) for lead in (0, 1)])
 
-    tn = (((0,), (0,)), ((), ()))
     top = coupled[...].astype(bf16)
     rest = (coupled[...] - top.astype(f32)).astype(bf16)
-    share[...] = lax.dot_general(own, top, tn, preferred_element_type=f32) + lax.dot_general(
-        own, rest, tn, preferred_element_type=f32
+    side = width // 2
+
+    def share_of(core):
+        left = own_t[pl.ds(pl.multiple_of(core * side, side), side), :]
+        return jnp.dot(left, top, preferred_element_type=f32) + jnp.dot(left, rest, preferred_element_type=f32)
+
+    share[...] = share_of(1 - c)
+    copy = pltpu.make_async_remote_copy(
+        src_ref=share, dst_ref=other, send_sem=core_send.at[0], recv_sem=core_recv.at[0],
+        device_id=shifted(1, 0), device_id_type=MESH,
     )
-
-    strip = width // PLANE
+    copy.start()
+    half_share = share_of(c)
+    copy.wait()
+    share[...] = half_share + other[...]
+
+    strip = side // PLANE
     copies = []
     for s in range(1, PLANE):
         device = shifted(0, s)
@@ -323,21 +347,22 @@
     for s, copy in enumerate(copies):
         copy.wait()
         total = total + reduce_in[s + 1]
-    column_in[f] = total
+    column_in[z] = total
     copies = []
-    for w in range(1, COLUMN):
-        copy = pltpu.make_async_remote_copy(
-            src_ref=column_in.at[f], dst_ref=column_in.at[f],
-            send_sem=column_send.at[w], recv_sem=column_recv.at[w], device_id=shifted(w, 0), device_id_type=MESH,
+    for step in range(1, SIDE):
+        copy = pltpu.make_async_remote_copy(
+            src_ref=column_in.at[z], dst_ref=column_in.at[z],
+            send_sem=column_send.at[step], recv_sem=column_recv.at[step],
+            device_id=shifted(2 * step, 0), device_id_type=MESH,
         )
         copy.start()
         copies.append(copy)
     for copy in copies:
         copy.wait()
     total = column_in[0]
-    for w in range(1, COLUMN):
-        total = total + column_in[w]
-    mine = pl.ds(pl.multiple_of(p * strip, strip), strip)
+    for step in range(1, SIDE):
+        total = total + column_in[step]
+    mine = pl.ds(pl.multiple_of(c * side + p * strip, strip), strip)
     full[mine, :] = total
     copies = []
     for s in range(1, PLANE):
@@ -349,7 +374,14 @@
         copies.append(copy)
     for copy in copies:
         copy.wait()
-    mass[...] = (full[...] + full[...].T) * factor
+    mine = pl.ds(pl.multiple_of(c * side, side), side)
+    copy = pltpu.make_async_remote_copy(
+        src_ref=full.at[mine], dst_ref=full.at[mine], send_sem=core_send.at[1], recv_sem=core_recv.at[1],
+        device_id=shifted(1, 0), device_id_type=MESH,
+    )
+    copy.start()
+    copy.wait()
+    mass[...] = full[...]
 
     everything = pl.ds(CAP, rows * 2 - CAP)
     pltpu.make_async_remote_copy(
@@ -364,16 +396,21 @@
     ).wait_send()
 
 
+def finish(factor, traces, summed, traces_out, mass):
+    traces_out[...] = traces[...]
+    mass[...] = (summed[...] + summed[...].T) * factor
+
+
 def shards(contributions, routes, slots, panels):
     rows, width = contributions.shape
     nodes = panels.shape[0]
     devices = lax.axis_size("fluid") * lax.axis_size("patch")
     bf16, f32, i32 = jnp.bfloat16, jnp.float32, jnp.int32
-    strip = width // PLANE
+    strip = width // 2 // PLANE
     vmem = pl.BlockSpec(memory_space=pltpu.VMEM)
     dma = pltpu.SemaphoreType.DMA
-    return pl.pallas_call(
-        functools.partial(kernel, 0.5 / math.sqrt(nodes * devices)),
+    summed = pl.pallas_call(
+        kernel,
         out_shape=(
             jax.ShapeDtypeStruct((nodes, width), bf16),
             jax.ShapeDtypeStruct((width, width), f32),
@@ -393,13 +430,16 @@
             pltpu.VMEM((PLANE, nodes, width), bf16),
             pltpu.VMEM((PLANE, nodes, nodes), bf16),
             pltpu.VMEM((nodes, width), f32),
+            pltpu.VMEM((width, nodes), bf16),
+            pltpu.VMEM((width // 2, width), f32),
+            pltpu.VMEM((width // 2, width), f32),
+            pltpu.VMEM((PLANE, strip, width), f32),
+            pltpu.VMEM((SIDE, strip, width), f32),
             pltpu.VMEM((width, width), f32),
-            pltpu.VMEM((PLANE, strip, width), f32),
-            pltpu.VMEM((COLUMN, strip, width), f32),
-            pltpu.VMEM((width, width), f32),
+            pltpu.SemaphoreType.REGULAR,
             dma, dma((PLANE,)), dma((COLUMN,)), dma((COLUMN,)), dma((PLANE,)), dma((PLANE,)),
             dma, dma((PLANE * 4,)), dma((PLANE,)),
-            dma((PLANE,)), dma((PLANE,)), dma((COLUMN,)), dma((COLUMN,)), dma((PLANE,)), dma((PLANE,)),
+            dma((2,)), dma((2,)), dma((PLANE,)), dma((PLANE,)), dma((SIDE,)), dma((SIDE,)), dma((PLANE,)), dma((PLANE,)),
         ],
         compiler_params=pltpu.CompilerParams(
             collective_id=0, has_side_effects=True, vmem_limit_bytes=60 * 1024 * 1024
@@ -408,6 +448,15 @@
             flops=2 * nodes * PLANE * nodes * width, bytes_accessed=nodes * nodes * PLANE * 2, transcendentals=0
         ),
     )(contributions, routes.reshape(1, rows), slots.reshape(1, rows), panels)
+    return pl.pallas_call(
+        functools.partial(finish, 0.5 / math.sqrt(nodes * devices)),
+        out_shape=(
+            jax.ShapeDtypeStruct((nodes, width), bf16),
+            jax.ShapeDtypeStruct((width, width), f32),
+        ),
+        in_specs=[vmem, vmem],
+        out_specs=(vmem, vmem),
+    )(*summed)
 
 
 def solution(mesh):

time: 106 us -> 101 us (0.953)
  local copies, waits for them, and re-layouts: 3.44 us -> 0 us
    unnamed x2 -> x0, local copies, waits for them, and re-layouts: 3.44 us -> none
    pallas_call x1 -> x2, Pallas kernels: 102 us -> 101 us  [the longest x1 98.7 us: shards(): pl.pallas_call(kernel, out_shape=(jax.ShapeDtypeStruct((nodes, width), bf...]
where the time goes in v2:
time: 101 us
  Pallas kernels  101 us (100%)
    pallas_call x1, Pallas kernels, shards(): pl.pallas_call(kernel, out_shape=(jax.ShapeDtypeStruct((nodes, width), bf...  98.7 us

profile of v2, /device:TPU:1, one launch (start us, length us, event | category | flops | bytes accessed | tf_op | source)
XLA Modules:
  0.0 101.3 jit_solution(3791957679681841688)
XLA Ops:
  0.6 98.7 %shard_map.59 = (bf16[768,256]{1,0:T(8,128)(2,1)}, f32[256,256]{1,0:T(8,128)}) custom-call(bf16[2048,256]{1,0:T(8,128)(2,1)} %contributions.1, s32[1,2048]{1,0:T(1,128)} %bitcast.2, s32[1,2048]{1,0:T(1,128)} %bitcast.3, bf16[768,12288]{1,0:T(8,128)(2,1)} %panels.1), custom_call_target="tpu_custom_call" | custom-call | flops 4831838208 | bytes 18874368 | tf_op jit(solution)/shard_map/pallas_call | solution.py:412
  99.3 2.0 %shard_map.60 = (bf16[768,256]{1,0:T(8,128)(2,1)}, f32[256,256]{1,0:T(8,128)}) custom-call(bf16[768,256]{1,0:T(8,128)(2,1)} %get-tuple-element.4.traces, f32[256,256]{1,0:T(8,128)} %get-tuple-element.5.summed), custom_call_target="tpu_custom_call" | custom-call | tf_op jit(solution)/shard_map/pallas_call | solution.py:451

commit v3 on v2

--- a/solution.py
+++ b/solution.py
@@ -34,16 +34,16 @@
 
 
 def kernel(
-    contributions, routes, slots, panels, traces, mass,
-    out_rows, in_rows, onehot, position, slot_out, column_slots, plane_out, plane_slots, landed,
-    gathered, panel_v, coupled, own_t, share, other, reduce_in, column_in, full, entered,
+    contributions_in, routes, slots, panels, traces, mass,
+    contributions, out_rows, in_rows, onehot, position, slot_out, column_slots, plane_out, plane_slots, landed,
+    gathered, panel_v, coupled, own_t, share, share_sent, reduce_in, column_in, full, entered,
     row_send, row_recv, slot_send, slot_recv, plane_send, plane_recv, gather_send, gather_recv, panel_sem,
-    core_send, core_recv, reduce_send, reduce_recv, column_send, column_recv, full_send, full_recv,
+    local_sem, reduce_send, reduce_recv, column_send, column_recv, full_send, full_recv,
 ):
     f32, bf16, i32 = jnp.float32, jnp.bfloat16, jnp.int32
     f, p = lax.axis_index("fluid"), lax.axis_index("patch")
     z, c, x, y = where_am_i()
-    rows = contributions.shape[0]
+    rows = contributions_in.shape[0]
     nodes = traces.shape[0]
     width = traces.shape[1]
     half, piece = nodes // 2, nodes // 4
@@ -54,6 +54,9 @@
         pl.semaphore_signal(barrier, inc=1, device_id=shifted(0, s), device_id_type=MESH)
     for w in range(1, COLUMN):
         pl.semaphore_signal(barrier, inc=1, device_id=shifted(w, 0), device_id_type=MESH)
+
+    rows_copy = pltpu.make_async_copy(contributions_in, contributions, local_sem.at[0])
+    rows_copy.start()
 
     panel_copies = []
     for s in range(PLANE):
@@ -92,6 +95,7 @@
     turn = (step_plane - STRIDE * step_column) & 15
     position[...] = (turn * COLUMN + step_column) * CAP + order
 
+    rows_copy.wait()
     pl.semaphore_wait(entered, COLUMN - 1)
 
     def build(kk):
@@ -252,7 +256,8 @@
         for direction in (1, -1):
             send_half(lead, lead, direction, (0, 0))
             send_half(lead, 1 - lead, direction, (0, 0))
-    traces[...] = own
+    traces_copy = pltpu.make_async_copy(gathered.at[0], traces, local_sem.at[1])
+    traces_copy.start()
     own_t[...] = own.T
     coupled[...] = jnp.zeros_like(coupled)
     for copy in panel_copies:
@@ -317,53 +322,41 @@
 
     top = coupled[...].astype(bf16)
     rest = (coupled[...] - top.astype(f32)).astype(bf16)
-    side = width // 2
-
-    def share_of(core):
-        left = own_t[pl.ds(pl.multiple_of(core * side, side), side), :]
-        return jnp.dot(left, top, preferred_element_type=f32) + jnp.dot(left, rest, preferred_element_type=f32)
-
-    share[...] = share_of(1 - c)
-    copy = pltpu.make_async_remote_copy(
-        src_ref=share, dst_ref=other, send_sem=core_send.at[0], recv_sem=core_recv.at[0],
-        device_id=shifted(1, 0), device_id_type=MESH,
+    share[...] = jnp.dot(own_t[...], top, preferred_element_type=f32) + jnp.dot(
+        own_t[...], rest, preferred_element_type=f32
     )
-    copy.start()
-    half_share = share_of(c)
-    copy.wait()
-    share[...] = half_share + other[...]
-
-    strip = side // PLANE
+    share_sent[...] = share[...].astype(bf16)
+
+    strip = width // PLANE
     copies = []
     for s in range(1, PLANE):
         device = shifted(0, s)
         copy = pltpu.make_async_remote_copy(
-            src_ref=share.at[pl.ds(pl.multiple_of(device[1] * strip, strip), strip)], dst_ref=reduce_in.at[s],
+            src_ref=share_sent.at[pl.ds(pl.multiple_of(device[1] * strip, strip), strip)], dst_ref=reduce_in.at[s],
             send_sem=reduce_send.at[s], recv_sem=reduce_recv.at[s], device_id=device, device_id_type=MESH,
         )
         copy.start()
         copies.append(copy)
-    total = share[pl.ds(pl.multiple_of(p * strip, strip), strip), :]
+    mine = pl.ds(pl.multiple_of(p * strip, strip), strip)
+    total = share[mine, :]
     for s, copy in enumerate(copies):
         copy.wait()
-        total = total + reduce_in[s + 1]
-    column_in[z] = total
+        total = total + reduce_in[s + 1].astype(f32)
+    column_in[f] = total.astype(bf16)
     copies = []
-    for step in range(1, SIDE):
-        copy = pltpu.make_async_remote_copy(
-            src_ref=column_in.at[z], dst_ref=column_in.at[z],
-            send_sem=column_send.at[step], recv_sem=column_recv.at[step],
-            device_id=shifted(2 * step, 0), device_id_type=MESH,
+    for w in range(1, COLUMN):
+        copy = pltpu.make_async_remote_copy(
+            src_ref=column_in.at[f], dst_ref=column_in.at[f],
+            send_sem=column_send.at[w], recv_sem=column_recv.at[w], device_id=shifted(w, 0), device_id_type=MESH,
         )
         copy.start()
         copies.append(copy)
     for copy in copies:
         copy.wait()
-    total = column_in[0]
-    for step in range(1, SIDE):
-        total = total + column_in[step]
-    mine = pl.ds(pl.multiple_of(c * side + p * strip, strip), strip)
-    full[mine, :] = total
+    total = column_in[0].astype(f32)
+    for w in range(1, COLUMN):
+        total = total + column_in[w].astype(f32)
+    full[mine, :] = total.astype(bf16)
     copies = []
     for s in range(1, PLANE):
         copy = pltpu.make_async_remote_copy(
@@ -374,14 +367,8 @@
         copies.append(copy)
     for copy in copies:
         copy.wait()
-    mine = pl.ds(pl.multiple_of(c * side, side), side)
-    copy = pltpu.make_async_remote_copy(
-        src_ref=full.at[mine], dst_ref=full.at[mine], send_sem=core_send.at[1], recv_sem=core_recv.at[1],
-        device_id=shifted(1, 0), device_id_type=MESH,
-    )
-    copy.start()
-    copy.wait()
     mass[...] = full[...]
+    traces_copy.wait()
 
     everything = pl.ds(CAP, rows * 2 - CAP)
     pltpu.make_async_remote_copy(
@@ -396,9 +383,12 @@
     ).wait_send()
 
 
-def finish(factor, traces, summed, traces_out, mass):
-    traces_out[...] = traces[...]
-    mass[...] = (summed[...] + summed[...].T) * factor
+def finish(factor, traces, summed, traces_out, mass, sem):
+    copy = pltpu.make_async_copy(traces, traces_out, sem)
+    copy.start()
+    wide = summed[...].astype(jnp.float32)
+    mass[...] = (wide + wide.T) * factor
+    copy.wait()
 
 
 def shards(contributions, routes, slots, panels):
@@ -406,18 +396,19 @@
     nodes = panels.shape[0]
     devices = lax.axis_size("fluid") * lax.axis_size("patch")
     bf16, f32, i32 = jnp.bfloat16, jnp.float32, jnp.int32
-    strip = width // 2 // PLANE
-    vmem = pl.BlockSpec(memory_space=pltpu.VMEM)
+    strip = width // PLANE
+    vmem, anywhere = pl.BlockSpec(memory_space=pltpu.VMEM), pl.BlockSpec(memory_space=pl.ANY)
     dma = pltpu.SemaphoreType.DMA
     summed = pl.pallas_call(
         kernel,
         out_shape=(
             jax.ShapeDtypeStruct((nodes, width), bf16),
-            jax.ShapeDtypeStruct((width, width), f32),
+            jax.ShapeDtypeStruct((width, width), bf16),
         ),
-        in_specs=[vmem, vmem, vmem, pl.BlockSpec(memory_space=pl.ANY)],
-        out_specs=(vmem, vmem),
+        in_specs=[anywhere, vmem, vmem, anywhere],
+        out_specs=(anywhere, vmem),
         scratch_shapes=[
+            pltpu.VMEM((rows, width), bf16),
             pltpu.VMEM((2 * rows, width), bf16),
             pltpu.VMEM((2 * rows, width), bf16),
             pltpu.VMEM((128, rows), bf16),
@@ -431,15 +422,15 @@
             pltpu.VMEM((PLANE, nodes, nodes), bf16),
             pltpu.VMEM((nodes, width), f32),
             pltpu.VMEM((width, nodes), bf16),
-            pltpu.VMEM((width // 2, width), f32),
-            pltpu.VMEM((width // 2, width), f32),
-            pltpu.VMEM((PLANE, strip, width), f32),
-            pltpu.VMEM((SIDE, strip, width), f32),
             pltpu.VMEM((width, width), f32),
+            pltpu.VMEM((width, width), bf16),
+            pltpu.VMEM((PLANE, strip, width), bf16),
+            pltpu.VMEM((COLUMN, strip, width), bf16),
+            pltpu.VMEM((width, width), bf16),
             pltpu.SemaphoreType.REGULAR,
             dma, dma((PLANE,)), dma((COLUMN,)), dma((COLUMN,)), dma((PLANE,)), dma((PLANE,)),
             dma, dma((PLANE * 4,)), dma((PLANE,)),
-            dma((2,)), dma((2,)), dma((PLANE,)), dma((PLANE,)), dma((SIDE,)), dma((SIDE,)), dma((PLANE,)), dma((PLANE,)),
+            dma((2,)), dma((PLANE,)), dma((PLANE,)), dma((COLUMN,)), dma((COLUMN,)), dma((PLANE,)), dma((PLANE,)),
         ],
         compiler_params=pltpu.CompilerParams(
             collective_id=0, has_side_effects=True, vmem_limit_bytes=60 * 1024 * 1024
@@ -454,8 +445,9 @@
             jax.ShapeDtypeStruct((nodes, width), bf16),
             jax.ShapeDtypeStruct((width, width), f32),
         ),
-        in_specs=[vmem, vmem],
-        out_specs=(vmem, vmem),
+        in_specs=[anywhere, vmem],
+        out_specs=(anywhere, vmem),
+        scratch_shapes=[dma],
     )(*summed)
 
 

time: 101 us -> 113 us (1.12)
  Pallas kernels: 101 us -> 112 us
    pallas_call x1, Pallas kernels: 1.99 us -> 14.6 us  [shards(): pl.pallas_call(functools.partial(finish, 0.5 / math.sqrt(nodes * devices)...]
    pallas_call x1, Pallas kernels: 98.7 us -> 97.5 us  [shards(): pl.pallas_call(kernel, out_shape=(jax.ShapeDtypeStruct((nodes, width), bf...]
where the time goes in v3:
time: 113 us
  Pallas kernels  112 us (99%)
    pallas_call x1, Pallas kernels, shards(): pl.pallas_call(kernel, out_shape=(jax.ShapeDtypeStruct((nodes, width), bf...  97.5 us
    pallas_call x1, Pallas kernels, shards(): pl.pallas_call(functools.partial(finish, 0.5 / math.sqrt(nodes * devices)...  14.6 us

profile of v3, /device:TPU:1, one launch (start us, length us, event | category | flops | bytes accessed | tf_op | source)
XLA Modules:
  0.0 112.7 jit_solution(6761311962030849287)
XLA Ops:
  0.6 97.5 %shard_map.59 = (bf16[768,256]{1,0:T(8,128)(2,1)}, bf16[256,256]{1,0:T(8,128)(2,1)}) custom-call(bf16[2048,256]{1,0:T(8,128)(2,1)} %contributions_in.1, s32[1,2048]{1,0:T(1,128)} %bitcast.2, s32[1,2048]{1,0:T(1,128)} %bitcast.3, bf16[768,12288]{1,0:T(8,128)(2,1)} %panels.1), custom_call_target="tpu_custom_call" | custom-call | flops 4831838208 | bytes 18874368 | tf_op jit(solution)/shard_map/pallas_call | solution.py:402
  98.1 14.6 %shard_map.60 = (bf16[768,256]{1,0:T(8,128)(2,1)}, f32[256,256]{1,0:T(8,128)}) custom-call(bf16[768,256]{1,0:T(8,128)(2,1)} %get-tuple-element.4.traces, bf16[256,256]{1,0:T(8,128)(2,1)} %get-tuple-element.5.summed), custom_call_target="tpu_custom_call" | custom-call | tf_op jit(solution)/shard_map/pallas_call | solution.py:442

commit v4 on v3

--- a/solution.py
+++ b/solution.py
@@ -58,16 +58,6 @@
     rows_copy = pltpu.make_async_copy(contributions_in, contributions, local_sem.at[0])
     rows_copy.start()
 
-    panel_copies = []
-    for s in range(PLANE):
-        dx, dy = s // SIDE, s % SIDE
-        owner = lax.rem(x + SIDE - dx, SIDE) * SIDE + lax.rem(y + SIDE - dy, SIDE)
-        copy = pltpu.make_async_copy(
-            panels.at[:, pl.ds(pl.multiple_of(owner * nodes, 128), nodes)], panel_v.at[s], panel_sem.at[s]
-        )
-        copy.start()
-        panel_copies.append(copy)
-
     to = routes[...]
     to_f, to_p = to >> 4, to & 15
     dz, dc = ((to_f >> 1) - z) & 3, ((to_f & 1) - c) & 1
@@ -95,31 +85,6 @@
     turn = (step_plane - STRIDE * step_column) & 15
     position[...] = (turn * COLUMN + step_column) * CAP + order
 
-    rows_copy.wait()
-    pl.semaphore_wait(entered, COLUMN - 1)
-
-    def build(kk):
-        i = lax.broadcasted_iota(i32, (256, 1), 0)
-        pick = (kk * 256 + i == position[...]).astype(bf16)
-        made = jnp.dot(pick, contributions[...], preferred_element_type=f32).astype(bf16)
-        out_rows[pl.ds(pl.multiple_of(kk * 256, 256), 256), :] = made
-
-    def row_copy(kk, w):
-        at = pl.ds(pl.multiple_of(kk * 256 + w * CAP, CAP), CAP)
-        return pltpu.make_async_remote_copy(
-            src_ref=out_rows.at[at], dst_ref=in_rows.at[at],
-            send_sem=row_send, recv_sem=row_recv.at[kk],
-            device_id=shifted(w, lax.rem(kk + STRIDE * w, PLANE)), device_id_type=MESH,
-        )
-
-    def send_rows(first, last):
-        @pl.loop(first, last)
-        def _(kk):
-            build(kk)
-            for w in range(COLUMN):
-                row_copy(kk, w).start()
-
-    send_rows(1, 3)
 
     value = slots[...] + 1
     lane_order = lax.broadcasted_iota(i32, (128, rows), 0) & (CAP - 1)
@@ -134,6 +99,30 @@
     slot_out[...] = jnp.where(lane_group == row_group, table, 0.0).astype(i32)
     column_slots[0] = slot_out[0:PLANE]
 
+    rows_copy.wait()
+    pl.semaphore_wait(entered, COLUMN - 1)
+
+    def build(kk):
+        i = lax.broadcasted_iota(i32, (256, 1), 0)
+        pick = (kk * 256 + i == position[...]).astype(bf16)
+        made = jnp.dot(pick, contributions[...], preferred_element_type=f32).astype(bf16)
+        out_rows[pl.ds(pl.multiple_of(kk * 256, 256), 256), :] = made
+
+    def row_copy(kk, w):
+        at = pl.ds(pl.multiple_of(kk * 256 + w * CAP, CAP), CAP)
+        return pltpu.make_async_remote_copy(
+            src_ref=out_rows.at[at], dst_ref=in_rows.at[at],
+            send_sem=row_send, recv_sem=row_recv.at[kk],
+            device_id=shifted(w, lax.rem(kk + STRIDE * w, PLANE)), device_id_type=MESH,
+        )
+
+    def send_rows(first, last):
+        @pl.loop(first, last)
+        def _(kk):
+            build(kk)
+            for w in range(COLUMN):
+                row_copy(kk, w).start()
+
     slot_copies = []
     for w in range(1, COLUMN):
         copy = pltpu.make_async_remote_copy(
@@ -143,7 +132,7 @@
         copy.start()
         slot_copies.append(copy)
 
-    send_rows(3, 9)
+    send_rows(1, 4)
 
     for copy in slot_copies:
         copy.wait()
@@ -161,11 +150,21 @@
         copy.start()
         plane_copies.append(copy)
 
-    send_rows(9, PLANE)
+    send_rows(4, PLANE)
     build(0)
     for w in range(1, COLUMN):
         row_copy(0, w).start()
     in_rows[0:CAP, :] = out_rows[0:CAP, :]
+
+    panel_copies = []
+    for s in range(PLANE):
+        dx, dy = s // SIDE, s % SIDE
+        owner = lax.rem(x + SIDE - dx, SIDE) * SIDE + lax.rem(y + SIDE - dy, SIDE)
+        copy = pltpu.make_async_copy(
+            panels.at[:, pl.ds(pl.multiple_of(owner * nodes, 128), nodes)], panel_v.at[s], panel_sem.at[s]
+        )
+        copy.start()
+        panel_copies.append(copy)
 
     for copy in plane_copies:
         copy.wait()
@@ -252,10 +251,10 @@
             panel_v[s, :, pl.ds(start, count)], gathered[s, pl.ds(start, count), :], preferred_element_type=f32
         )
 
-    for lead in (0, 1):
+    for turned in (0, 1):
         for direction in (1, -1):
-            send_half(lead, lead, direction, (0, 0))
-            send_half(lead, 1 - lead, direction, (0, 0))
+            for lead in (0, 1):
+                send_half(lead, lead ^ turned, direction, (0, 0))
     traces_copy = pltpu.make_async_copy(gathered.at[0], traces, local_sem.at[1])
     traces_copy.start()
     own_t[...] = own.T
@@ -275,19 +274,19 @@
             send_piece(lead, lead, direction, place, k)
             send_half(lead, 1 - lead, 1, place)
             send_half(lead, 1 - lead, -1, place)
-    for k, b, direction in ((0, 1, 1), (1, 3, -1)):
-        for lead in (0, 1):
-            place = at(lead, 0, b)
-            wait_half(lead, place)
-            send_piece(lead, 1 - lead, direction, place, k)
-    multiply_halves([(lead, at(lead, a, b)) for a, b in ((1, 0), (3, 0), (0, 1), (0, 3)) for lead in (0, 1)])
+    multiply_halves([(lead, at(lead, a, 0)) for a in (1, 3) for lead in (0, 1)])
     for k in (0, 1):
         for lead in (0, 1):
             place = at(lead, 2, 0)
             wait_piece(lead, place, k)
             send_piece(lead, 1 - lead, 1, place, k)
             send_piece(lead, 1 - lead, -1, place, k)
-    multiply_halves([(lead, at(lead, 2, 0)) for lead in (0, 1)])
+    for k, b, direction in ((0, 1, 1), (1, 3, -1)):
+        for lead in (0, 1):
+            place = at(lead, 0, b)
+            wait_half(lead, place)
+            send_piece(lead, 1 - lead, direction, place, k)
+    multiply_halves([(lead, at(lead, a, b)) for a, b in ((2, 0), (0, 1), (0, 3)) for lead in (0, 1)])
     for a in (1, 3):
         for k, b, direction in ((0, 1, 1), (1, 3, -1)):
             for lead in (0, 1):
@@ -383,12 +382,10 @@
     ).wait_send()
 
 
-def finish(factor, traces, summed, traces_out, mass, sem):
-    copy = pltpu.make_async_copy(traces, traces_out, sem)
-    copy.start()
+def finish(factor, traces, summed, traces_out, mass):
+    traces_out[...] = traces[...]
     wide = summed[...].astype(jnp.float32)
     mass[...] = (wide + wide.T) * factor
-    copy.wait()
 
 
 def shards(contributions, routes, slots, panels):
@@ -445,9 +442,8 @@
             jax.ShapeDtypeStruct((nodes, width), bf16),
             jax.ShapeDtypeStruct((width, width), f32),
         ),
-        in_specs=[anywhere, vmem],
-        out_specs=(anywhere, vmem),
-        scratch_shapes=[dma],
+        in_specs=[vmem, vmem],
+        out_specs=(vmem, vmem),
     )(*summed)
 
 

time: 113 us -> 94.4 us (0.84)
  Pallas kernels: 112 us -> 93.5 us
    pallas_call x1, Pallas kernels: 14.6 us -> 1.9 us  [shards(): pl.pallas_call(functools.partial(finish, 0.5 / math.sqrt(nodes * devices)...]
    pallas_call x1, Pallas kernels: 97.5 us -> 91.6 us  [shards(): pl.pallas_call(kernel, out_shape=(jax.ShapeDtypeStruct((nodes, width), bf...]
where the time goes in v4:
time: 94.4 us; the launch traced here: 94.2 us
  Pallas kernels  93.5 us (99%)
    pallas_call x1, Pallas kernels, shards(): pl.pallas_call(kernel, out_shape=(jax.ShapeDtypeStruct((nodes, width), bf...  91.6 us
    pallas_call x1, Pallas kernels, shards(): pl.pallas_call(functools.partial(finish, 0.5 / math.sqrt(nodes * devices)...  1.9 us

profile of v4, /device:TPU:1, one launch (start us, length us, event | category | flops | bytes accessed | tf_op | source)
XLA Modules:
  0.0 94.2 jit_solution(14970115426254226532)
XLA Ops:
  0.6 91.6 %shard_map.59 = (bf16[768,256]{1,0:T(8,128)(2,1)}, bf16[256,256]{1,0:T(8,128)(2,1)}) custom-call(bf16[2048,256]{1,0:T(8,128)(2,1)} %contributions_in.1, s32[1,2048]{1,0:T(1,128)} %bitcast.2, s32[1,2048]{1,0:T(1,128)} %bitcast.3, bf16[768,12288]{1,0:T(8,128)(2,1)} %panels.1), custom_call_target="tpu_custom_call" | custom-call | flops 4831838208 | bytes 18874368 | tf_op jit(solution)/shard_map/pallas_call | solution.py:399
  92.3 1.9 %shard_map.60 = (bf16[768,256]{1,0:T(8,128)(2,1)}, f32[256,256]{1,0:T(8,128)}) custom-call(bf16[768,256]{1,0:T(8,128)(2,1)} %get-tuple-element.4.traces, bf16[256,256]{1,0:T(8,128)(2,1)} %get-tuple-element.5.summed), custom_call_target="tpu_custom_call" | custom-call | tf_op jit(solution)/shard_map/pallas_call | solution.py:439

commit v5 on v4

--- a/solution.py
+++ b/solution.py
@@ -13,7 +13,10 @@
 COLUMN = 8
 PLANE = 16
 CAP = 32
+SLOT_BITS = 10
 STRIDE = 5
+PLANE_PEERS = (10, 9, 11, 6, 14, 2, 8, 5, 7, 13, 15, 1, 3, 4, 12)
+COLUMN_PEERS = (5, 4, 3, 7, 2, 6, 1)
 
 
 def where_am_i():
@@ -34,11 +37,11 @@
 
 
 def kernel(
-    contributions_in, routes, slots, panels, traces, mass,
+    contributions_in, names_in, panels, traces, mass,
     contributions, out_rows, in_rows, onehot, position, slot_out, column_slots, plane_out, plane_slots, landed,
     gathered, panel_v, coupled, own_t, share, share_sent, reduce_in, column_in, full, entered,
     row_send, row_recv, slot_send, slot_recv, plane_send, plane_recv, gather_send, gather_recv, panel_sem,
-    local_sem, reduce_send, reduce_recv, column_send, column_recv, full_send, full_recv,
+    operand_sem, local_sem, reduce_send, reduce_recv, column_send, column_recv, full_send, full_recv,
 ):
     f32, bf16, i32 = jnp.float32, jnp.bfloat16, jnp.int32
     f, p = lax.axis_index("fluid"), lax.axis_index("patch")
@@ -48,17 +51,17 @@
     width = traces.shape[1]
     half, piece = nodes // 2, nodes // 4
 
+    rows_copy = pltpu.make_async_copy(contributions_in, contributions, operand_sem)
+    rows_copy.start()
+
     barrier = pltpu.get_barrier_semaphore()
 
-    for s in range(1, PLANE):
+    for s in PLANE_PEERS:
         pl.semaphore_signal(barrier, inc=1, device_id=shifted(0, s), device_id_type=MESH)
-    for w in range(1, COLUMN):
+    for w in COLUMN_PEERS:
         pl.semaphore_signal(barrier, inc=1, device_id=shifted(w, 0), device_id_type=MESH)
 
-    rows_copy = pltpu.make_async_copy(contributions_in, contributions, local_sem.at[0])
-    rows_copy.start()
-
-    to = routes[...]
+    to = names_in[...] >> SLOT_BITS
     to_f, to_p = to >> 4, to & 15
     dz, dc = ((to_f >> 1) - z) & 3, ((to_f & 1) - c) & 1
     dx, dy = ((to_p >> 2) - x) & 3, ((to_p & 3) - y) & 3
@@ -67,7 +70,7 @@
     onehot[...] = (lax.broadcasted_iota(i32, (128, rows), 0) == label).astype(bf16)
     block = 256
     pl.semaphore_wait(barrier, PLANE + COLUMN - 2)
-    for w in range(1, COLUMN):
+    for w in COLUMN_PEERS:
         pl.semaphore_signal(entered, inc=1, device_id=shifted(w, 0), device_id_type=MESH)
 
     upper = (
@@ -85,8 +88,7 @@
     turn = (step_plane - STRIDE * step_column) & 15
     position[...] = (turn * COLUMN + step_column) * CAP + order
 
-
-    value = slots[...] + 1
+    value = (names_in[...] & ((1 << SLOT_BITS) - 1)) + 1
     lane_order = lax.broadcasted_iota(i32, (128, rows), 0) & (CAP - 1)
     hit = lane_order == order
     nt = (((1,), (1,)), ((), ()))
@@ -100,13 +102,20 @@
     column_slots[0] = slot_out[0:PLANE]
 
     rows_copy.wait()
-    pl.semaphore_wait(entered, COLUMN - 1)
+
+    def picked(rows_wanted):
+        pick = (rows_wanted == position[...]).astype(bf16)
+        return jnp.dot(pick, contributions[...], preferred_element_type=f32).astype(bf16)
+
+    def build_plane(first):
+        i = lax.broadcasted_iota(i32, (256, 1), 0)
+        made = picked((first + (i >> 5)) * 256 + (i & 31))
+        for k in range(8):
+            out_rows[(first + k) * 256:(first + k) * 256 + CAP, :] = made[k * CAP:(k + 1) * CAP]
 
     def build(kk):
-        i = lax.broadcasted_iota(i32, (256, 1), 0)
-        pick = (kk * 256 + i == position[...]).astype(bf16)
-        made = jnp.dot(pick, contributions[...], preferred_element_type=f32).astype(bf16)
-        out_rows[pl.ds(pl.multiple_of(kk * 256, 256), 256), :] = made
+        i = lax.broadcasted_iota(i32, (256 - CAP, 1), 0)
+        out_rows[pl.ds(pl.multiple_of(kk * 256 + CAP, CAP), 256 - CAP), :] = picked(kk * 256 + CAP + i)
 
     def row_copy(kk, w):
         at = pl.ds(pl.multiple_of(kk * 256 + w * CAP, CAP), CAP)
@@ -120,11 +129,11 @@
         @pl.loop(first, last)
         def _(kk):
             build(kk)
-            for w in range(COLUMN):
+            for w in range(1, COLUMN):
                 row_copy(kk, w).start()
 
     slot_copies = []
-    for w in range(1, COLUMN):
+    for w in COLUMN_PEERS:
         copy = pltpu.make_async_remote_copy(
             src_ref=slot_out.at[pl.ds(w * PLANE, PLANE)], dst_ref=column_slots.at[w],
             send_sem=slot_send.at[w], recv_sem=slot_recv.at[w], device_id=shifted(w, 0), device_id_type=MESH,
@@ -132,6 +141,13 @@
         copy.start()
         slot_copies.append(copy)
 
+    for first in (8, 0):
+        build_plane(first)
+        for kk in range(first, first + 8):
+            if kk > 0:
+                row_copy(kk, 0).start()
+
+    pl.semaphore_wait(entered, COLUMN - 1)
     send_rows(1, 4)
 
     for copy in slot_copies:
@@ -142,7 +158,7 @@
     plane_out[...] = jnp.where(sub < 4, first[:, None, :], second[:, None, :])
     plane_slots[0] = plane_out[0]
     plane_copies = []
-    for s in range(1, PLANE):
+    for s in PLANE_PEERS:
         copy = pltpu.make_async_remote_copy(
             src_ref=plane_out.at[s], dst_ref=plane_slots.at[s],
             send_sem=plane_send.at[s], recv_sem=plane_recv.at[s], device_id=shifted(0, s), device_id_type=MESH,
@@ -255,7 +271,7 @@
         for direction in (1, -1):
             for lead in (0, 1):
                 send_half(lead, lead ^ turned, direction, (0, 0))
-    traces_copy = pltpu.make_async_copy(gathered.at[0], traces, local_sem.at[1])
+    traces_copy = pltpu.make_async_copy(gathered.at[0], traces, local_sem)
     traces_copy.start()
     own_t[...] = own.T
     coupled[...] = jnp.zeros_like(coupled)
@@ -317,18 +333,24 @@
     for k in (0, 1):
         for lead in (0, 1):
             wait_piece(lead, at(lead, 2, 2), k)
-    multiply_halves([(lead, at(lead, 2, 2)) for lead in (0, 1)])
-
-    top = coupled[...].astype(bf16)
-    rest = (coupled[...] - top.astype(f32)).astype(bf16)
-    share[...] = jnp.dot(own_t[...], top, preferred_element_type=f32) + jnp.dot(
-        own_t[...], rest, preferred_element_type=f32
-    )
+
+    last = 2 * SIDE + 2
+    total = jnp.zeros((width, width), f32)
+    for r in range(0, nodes, 256):
+        wide = coupled[r:r + 256, :] + jnp.dot(
+            panel_v[last, r:r + 256, :], gathered[last], preferred_element_type=f32
+        )
+        top = wide.astype(bf16)
+        rest = (wide - top.astype(f32)).astype(bf16)
+        left = own_t[:, r:r + 256]
+        total = total + jnp.dot(left, top, preferred_element_type=f32)
+        total = total + jnp.dot(left, rest, preferred_element_type=f32)
+    share[...] = total
     share_sent[...] = share[...].astype(bf16)
 
     strip = width // PLANE
     copies = []
-    for s in range(1, PLANE):
+    for s in PLANE_PEERS:
         device = shifted(0, s)
         copy = pltpu.make_async_remote_copy(
             src_ref=share_sent.at[pl.ds(pl.multiple_of(device[1] * strip, strip), strip)], dst_ref=reduce_in.at[s],
@@ -338,12 +360,13 @@
         copies.append(copy)
     mine = pl.ds(pl.multiple_of(p * strip, strip), strip)
     total = share[mine, :]
-    for s, copy in enumerate(copies):
-        copy.wait()
-        total = total + reduce_in[s + 1].astype(f32)
+    for copy in copies:
+        copy.wait()
+    for s in range(1, PLANE):
+        total = total + reduce_in[s].astype(f32)
     column_in[f] = total.astype(bf16)
     copies = []
-    for w in range(1, COLUMN):
+    for w in COLUMN_PEERS:
         copy = pltpu.make_async_remote_copy(
             src_ref=column_in.at[f], dst_ref=column_in.at[f],
             send_sem=column_send.at[w], recv_sem=column_recv.at[w], device_id=shifted(w, 0), device_id_type=MESH,
@@ -357,7 +380,7 @@
         total = total + column_in[w].astype(f32)
     full[mine, :] = total.astype(bf16)
     copies = []
-    for s in range(1, PLANE):
+    for s in PLANE_PEERS:
         copy = pltpu.make_async_remote_copy(
             src_ref=full.at[mine], dst_ref=full.at[mine],
             send_sem=full_send.at[s], recv_sem=full_recv.at[s], device_id=shifted(0, s), device_id_type=MESH,
@@ -395,14 +418,16 @@
     bf16, f32, i32 = jnp.bfloat16, jnp.float32, jnp.int32
     strip = width // PLANE
     vmem, anywhere = pl.BlockSpec(memory_space=pltpu.VMEM), pl.BlockSpec(memory_space=pl.ANY)
+    hbm = pl.BlockSpec(memory_space=pltpu.HBM)
     dma = pltpu.SemaphoreType.DMA
+    names = (routes * (1 << SLOT_BITS) + slots.reshape(rows, 1)).reshape(1, rows)
     summed = pl.pallas_call(
         kernel,
         out_shape=(
             jax.ShapeDtypeStruct((nodes, width), bf16),
             jax.ShapeDtypeStruct((width, width), bf16),
         ),
-        in_specs=[anywhere, vmem, vmem, anywhere],
+        in_specs=[hbm, vmem, hbm],
         out_specs=(anywhere, vmem),
         scratch_shapes=[
             pltpu.VMEM((rows, width), bf16),
@@ -427,15 +452,15 @@
             pltpu.SemaphoreType.REGULAR,
             dma, dma((PLANE,)), dma((COLUMN,)), dma((COLUMN,)), dma((PLANE,)), dma((PLANE,)),
             dma, dma((PLANE * 4,)), dma((PLANE,)),
-            dma((2,)), dma((PLANE,)), dma((PLANE,)), dma((COLUMN,)), dma((COLUMN,)), dma((PLANE,)), dma((PLANE,)),
+            dma, dma, dma((PLANE,)), dma((PLANE,)), dma((COLUMN,)), dma((COLUMN,)), dma((PLANE,)), dma((PLANE,)),
         ],
         compiler_params=pltpu.CompilerParams(
-            collective_id=0, has_side_effects=True, vmem_limit_bytes=60 * 1024 * 1024
+            collective_id=0, has_side_effects=True, vmem_limit_bytes=53 * 1024 * 1024
         ),
         cost_estimate=pl.CostEstimate(
             flops=2 * nodes * PLANE * nodes * width, bytes_accessed=nodes * nodes * PLANE * 2, transcendentals=0
         ),
-    )(contributions, routes.reshape(1, rows), slots.reshape(1, rows), panels)
+    )(contributions, names, panels)
     return pl.pallas_call(
         functools.partial(finish, 0.5 / math.sqrt(nodes * devices)),
         out_shape=(
@@ -444,6 +469,7 @@
         ),
         in_specs=[vmem, vmem],
         out_specs=(vmem, vmem),
+        compiler_params=pltpu.CompilerParams(vmem_limit_bytes=4 * 1024 * 1024),
     )(*summed)
 
 

time: 94.4 us -> 92.3 us (0.978)
  Pallas kernels: 93.5 us -> 90.7 us
    pallas_call x1, Pallas kernels: 91.6 us -> 89.8 us  [shards(): pl.pallas_call(kernel, out_shape=(jax.ShapeDtypeStruct((nodes, width), bf...]
    pallas_call x1, Pallas kernels: 1.9 us -> 0.89 us  [shards(): pl.pallas_call(functools.partial(finish, 0.5 / math.sqrt(nodes * devices)...]
where the time goes in v5:
time: 92.3 us; the launch traced here: 92.1 us
  Pallas kernels  90.7 us (98%)
    pallas_call x1, Pallas kernels, shards(): pl.pallas_call(kernel, out_shape=(jax.ShapeDtypeStruct((nodes, width), bf...  89.8 us

profile of v5, /device:TPU:1, one launch (start us, length us, event | category | flops | bytes accessed | tf_op | source)
XLA Modules:
  0.0 92.1 jit_solution(18353331455810889073)
XLA Ops:
  0.6 0.7 add_bitcast_fusion.names_in
  1.4 89.8 %shard_map.59 = (bf16[768,256]{1,0:T(8,128)(2,1)S(1)}, bf16[256,256]{1,0:T(8,128)(2,1)S(1)}) custom-call(bf16[2048,256]{1,0:T(8,128)(2,1)} %contributions_in.1, s32[1,2048]{1,0:T(1,128)S(1)} %add_bitcast_fusion.names_in, bf16[768,12288]{1,0:T(8,128)(2,1)} %panels.1), custom_call_target="tpu_custom_call" | custom-call | flops 4831838208 | bytes 18874368 | tf_op jit(solution)/shard_map/pallas_call | solution.py:424
  91.2 0.9 shard_map.60

commit v6 on v5

--- a/solution.py
+++ b/solution.py
@@ -14,7 +14,7 @@
 PLANE = 16
 CAP = 32
 SLOT_BITS = 10
-STRIDE = 5
+STRIDE = 7
 PLANE_PEERS = (10, 9, 11, 6, 14, 2, 8, 5, 7, 13, 15, 1, 3, 4, 12)
 COLUMN_PEERS = (5, 4, 3, 7, 2, 6, 1)
 
@@ -34,6 +34,12 @@
         lax.rem(z + dz, SIDE) * 2 + lax.rem(c + dc, 2),
         lax.rem(x + dx, SIDE) * SIDE + lax.rem(y + dy, SIDE),
     )
+
+
+def plane_step_of(turn, w):
+    if isinstance(turn, int) and turn == 0:
+        return 0
+    return lax.rem(turn - 1 + STRIDE * w % (PLANE - 1), PLANE - 1) + 1
 
 
 def kernel(
@@ -85,7 +91,10 @@
         orders.append(jnp.sum(wide * before, axis=0, keepdims=True))
         seen = seen + jnp.sum(wide, axis=1, keepdims=True)
     order = jnp.concatenate(orders, axis=1).astype(i32)
-    turn = (step_plane - STRIDE * step_column) & 15
+    turn = step_plane - STRIDE * step_column
+    for _ in range(STRIDE * (COLUMN - 1) // (PLANE - 1) + 1):
+        turn = jnp.where(turn < 1, turn + (PLANE - 1), turn)
+    turn = jnp.where(step_plane == 0, 0, turn)
     position[...] = (turn * COLUMN + step_column) * CAP + order
 
     value = (names_in[...] & ((1 << SLOT_BITS) - 1)) + 1
@@ -122,7 +131,7 @@
         return pltpu.make_async_remote_copy(
             src_ref=out_rows.at[at], dst_ref=in_rows.at[at],
             send_sem=row_send, recv_sem=row_recv.at[kk],
-            device_id=shifted(w, lax.rem(kk + STRIDE * w, PLANE)), device_id_type=MESH,
+            device_id=shifted(w, plane_step_of(kk, w)), device_id_type=MESH,
         )
 
     def send_rows(first, last):
@@ -141,6 +150,9 @@
         copy.start()
         slot_copies.append(copy)
 
+    build(0)
+    for w in COLUMN_PEERS:
+        row_copy(0, w).start()
     for first in (8, 0):
         build_plane(first)
         for kk in range(first, first + 8):
@@ -167,9 +179,6 @@
         plane_copies.append(copy)
 
     send_rows(4, PLANE)
-    build(0)
-    for w in range(1, COLUMN):
-        row_copy(0, w).start()
     in_rows[0:CAP, :] = out_rows[0:CAP, :]
 
     panel_copies = []
@@ -194,7 +203,7 @@
             row = jnp.zeros((1, 128), i32)
             for k in range(4):
                 w = side * 4 + k
-                got = plane_slots[lax.rem(kk + STRIDE * w, PLANE), pl.ds(side * 4, 1), :]
+                got = plane_slots[plane_step_of(kk, w), pl.ds(side * 4, 1), :]
                 row = row + jnp.where(group == k, got, 0)
             parts.append(row)
         names = jnp.concatenate(parts, axis=1) - 1
@@ -210,13 +219,14 @@
             send_sem=row_send, recv_sem=row_recv.at[kk], device_id=(f, p), device_id_type=MESH,
         )
 
+    arrival(0, CAP, 256 - CAP).wait_recv()
+    land(0)
+
     @pl.loop(1, PLANE)
     def _(kk):
         arrival(kk, pl.multiple_of(kk * 256, 256), 256).wait_recv()
         land(kk)
 
-    arrival(0, CAP, 256 - CAP).wait_recv()
-    land(0)
     own = landed[...].astype(bf16)
     gathered[0] = own
 

time: 92.3 us -> 91.3 us (0.989)
  Pallas kernels: 90.7 us -> 89.7 us
    pallas_call x1, Pallas kernels: 89.8 us -> 88.9 us  [shards(): pl.pallas_call(kernel, out_shape=(jax.ShapeDtypeStruct((nodes, width), bf...]
where the time goes in v6:
time: 91.3 us; the launch traced here: 91.1 us
  Pallas kernels  89.7 us (98%)
    pallas_call x1, Pallas kernels, shards(): pl.pallas_call(kernel, out_shape=(jax.ShapeDtypeStruct((nodes, width), bf...  88.9 us

profile of v6, /device:TPU:1, one launch (start us, length us, event | category | flops | bytes accessed | tf_op | source)
XLA Modules:
  0.0 91.1 jit_solution(15862324599812195658)
XLA Ops:
  0.6 0.7 add_bitcast_fusion.names_in
  1.4 88.9 %shard_map.59 = (bf16[768,256]{1,0:T(8,128)(2,1)S(1)}, bf16[256,256]{1,0:T(8,128)(2,1)S(1)}) custom-call(bf16[2048,256]{1,0:T(8,128)(2,1)} %contributions_in.1, s32[1,2048]{1,0:T(1,128)S(1)} %add_bitcast_fusion.names_in, bf16[768,12288]{1,0:T(8,128)(2,1)} %panels.1), custom_call_target="tpu_custom_call" | custom-call | flops 4831838208 | bytes 18874368 | tf_op jit(solution)/shard_map/pallas_call | solution.py:434
  90.2 0.9 shard_map.60

commit v7 on v6

--- a/solution.py
+++ b/solution.py
@@ -227,8 +227,6 @@
         arrival(kk, pl.multiple_of(kk * 256, 256), 256).wait_recv()
         land(kk)
 
-    own = landed[...].astype(bf16)
-    gathered[0] = own
 
     sent = []
 
@@ -277,13 +275,17 @@
             panel_v[s, :, pl.ds(start, count)], gathered[s, pl.ds(start, count), :], preferred_element_type=f32
         )
 
-    for turned in (0, 1):
+    for lead in (0, 1):
+        ready = slice(lead * half, (lead + 1) * half)
+        gathered[0, ready, :] = landed[ready, :].astype(bf16)
         for direction in (1, -1):
-            for lead in (0, 1):
-                send_half(lead, lead ^ turned, direction, (0, 0))
+            send_half(lead, lead, direction, (0, 0))
+    for direction in (1, -1):
+        for lead in (0, 1):
+            send_half(lead, 1 - lead, direction, (0, 0))
     traces_copy = pltpu.make_async_copy(gathered.at[0], traces, local_sem)
     traces_copy.start()
-    own_t[...] = own.T
+    own_t[...] = gathered[0].T
     coupled[...] = jnp.zeros_like(coupled)
     for copy in panel_copies:
         copy.wait()

time: 91.3 us -> 91.3 us (level)
  no operation moved by 1% of the time
where the time goes in v7:
time: 91.3 us; the launch traced here: 91.1 us
  Pallas kernels  89.7 us (98%)
    pallas_call x1, Pallas kernels, shards(): pl.pallas_call(kernel, out_shape=(jax.ShapeDtypeStruct((nodes, width), bf...  88.8 us

profile of v7, /device:TPU:1, one launch (start us, length us, event | category | flops | bytes accessed | tf_op | source)
XLA Modules:
  0.0 91.1 jit_solution(6542027328355880741)
XLA Ops:
  0.6 0.7 add_bitcast_fusion.names_in
  1.4 88.8 %shard_map.59 = (bf16[768,256]{1,0:T(8,128)(2,1)S(1)}, bf16[256,256]{1,0:T(8,128)(2,1)S(1)}) custom-call(bf16[2048,256]{1,0:T(8,128)(2,1)} %contributions_in.1, s32[1,2048]{1,0:T(1,128)S(1)} %add_bitcast_fusion.names_in, bf16[768,12288]{1,0:T(8,128)(2,1)} %panels.1), custom_call_target="tpu_custom_call" | custom-call | flops 4831838208 | bytes 18874368 | tf_op jit(solution)/shard_map/pallas_call | solution.py:436
  90.2 0.9 shard_map.60
